TPU v7x, 512 devices: a whole 4x4x16 slice. The times are simulated.
512 devices in a mesh: tm: 32 (over z_lo, y), feat: 16 (over x, z_hi, core).
Axes of the slice: x: 4, y: 4, z: 16 (z_hi: 2, z_lo: 8; z = z_hi * 8 + z_lo), core: 2. Of those that a mesh axis runs over, the one named last changes fastest.
Arguments:
- frames: bfloat16 [24576, 8192], P('tm', 'feat'), may hold values from -6 to 6
Outputs:
- instant: float32 [8192, 2, 512], P(('feat', 'tm'))
- lagged_cov: float32 [8192, 2, 512], P(('feat', 'tm'))
All inputs are finite; a program needn't handle non-finite values.
Results may differ from a plain program's by a relative error of at most 0.0003.
Values may be sent and summed in bfloat16 or wider, within the bound.
A program may use at most 64 MiB of HBM per device.

v0:
```python
import math

import jax
import jax.numpy as jnp
from jax import lax
from jax.sharding import Mesh
from jax.sharding import PartitionSpec as P

LAG = 256
STEPS = 2
TM = ("tm_0", "tm_1")
FEAT_TM = ("feat", "tm_0", "tm_1")


def shifted_2(shard, axis, by):
    peers = lax.axis_size(axis)
    pairs = [(i, i + by) for i in range(peers) if 0 <= i + by < peers]
    return lax.ppermute(shard, axis, pairs)


def passed_along(shard, axis, by):
    peers = lax.axis_size(axis)
    return lax.ppermute(shard, axis, [(i, (i + by) % peers) for i in range(peers)])


def own_block(parts, axes, sequence):
    shape = [lax.axis_size(a) for a in axes]
    parts = parts.reshape(*shape, *parts.shape[1:])
    parts = parts.transpose(*sequence, *range(len(axes), parts.ndim))
    parts = parts.reshape(-1, *parts.shape[len(axes) :])
    for k in sequence:
        parts = lax.psum_scatter(parts, axes[k], scatter_dimension=0, tiled=True)
    return parts[0]


def in_blocks(shard, dim, peers):
    before, after = (shard.shape[:dim], shard.shape[dim + 1 :])
    return jnp.moveaxis(shard.reshape(*before, peers, -1, *after), dim, 0)


def scatter_axes(shard, axes, sequence, dim):
    peers = lax.axis_size(axes)
    return own_block(in_blocks(shard, dim, peers), axes, sequence)


def one_tile(columns, other, norm_scale):
    dims = (((0,), (0,)), ((), ()))
    return lax.dot_general(columns, other, dims, preferred_element_type=jnp.float32) * norm_scale


def pair_tiles(columns, current, shifted, norm_scale):
    return jnp.stack(
        [one_tile(columns, current, norm_scale), one_tile(columns, shifted, norm_scale)], axis=1
    )


def shards(frames):
    rows_here, panel_width = frames.shape
    count_tm = lax.axis_size(TM)
    norm_scale = 1.0 / math.sqrt(rows_here * count_tm)
    currents = []
    lagged = []
    tail_rows = shifted_2(frames[:LAG], TM, -1)
    longer = jnp.concatenate([frames, tail_rows], axis=0)
    for step in range(STEPS):
        if step > 0:
            longer = passed_along(longer, "feat", -1)
        currents.append(longer[:rows_here])
        lagged.append(longer[LAG:])
    result = scatter_axes(
        jnp.stack(
            [pair_tiles(frames, currents[step], lagged[step], norm_scale) for step in range(STEPS)],
            axis=2,
        ),
        TM,
        (1, 0),
        0,
    )
    return (result[:, 0], result[:, 1])


def solution(mesh):
    split = Mesh(mesh.devices.reshape(8, 4, mesh.shape["feat"]), ("tm_0", "tm_1", "feat"))
    placed = (P(TM, "feat"),)
    return jax.shard_map(
        shards,
        mesh=split,
        in_specs=placed,
        out_specs=(P(FEAT_TM, None, None), P(FEAT_TM, None, None)),
        check_vma=False,
    )
```

profile of v0, /device:TPU:6, one launch (start us, length us, event | category | flops | bytes accessed | tf_op | source)
XLA Modules:
  0.0 231.3 jit_solution(11609273327575035487)
XLA Ops:
  7.2 0.0 copy-start
  7.2 0.0 reduce-scatter.3.cloned.1.call-start
  7.2 1.0 slice.18
  8.3 1.3 collective-permute-start
  9.6 2.1 constant_dynamic-update-slice_fusion.1
  11.6 6.6 %collective-permute-done = bf16[256,512]{1,0:T(8,128)(2,1)S(1)} collective-permute-done((bf16[256,512]{1,0:T(8,128)(2,1)S(1)}, bf16[256,512]{1,0:T(8,128)(2,1)S(1)}, u32[]{:S(2)}, u32[]{:S(2)}) %collective-permute-start) | collective-permute-done | bytes 262176 | tf_op jit(solution)/shard_map/ppermute | solution.py:18
  18.2 0.7 constant_dynamic-update-slice_fusion
  18.9 14.5 %collective-permute-start.1 = (bf16[1024,512]{1,0:T(8,128)(2,1)}, bf16[1024,512]{1,0:T(8,128)(2,1)}, u32[]{:S(2)}, u32[]{:S(2)}) collective-permute-start(bf16[1024,512]{1,0:T(8,128)(2,1)} %constant_dynamic-update-slice_fusion), channel_id=1, source_target_pairs={{0,15},{1,0},{2,1},{3,2},{4,3},{5,4},{6,5},{7,6},{8,7},{9,8},{10,9... | collective-permute-start | bytes 3145736 | tf_op jit(solution)/shard_map/ppermute | solution.py:23
  33.5 3.0 %convolution_multiply_fusion.3 = f32[512,512]{1,0:T(8,128)} fusion(bf16[768,512]{1,0:T(8,128)(2,1)} %param.1), kind=kOutput, calls=%fused_computation.7 | convolution fusion | flops 402915328 | bytes 1835008 | tf_op jit(solution)/shard_map/dot_general | solution.py:48
  36.5 0.0 copy-done
  36.5 1.7 fusion.2
  38.2 0.3 copy.17
  38.5 12.3 %collective-permute-done.1 = bf16[1024,512]{1,0:T(8,128)(2,1)} collective-permute-done((bf16[1024,512]{1,0:T(8,128)(2,1)}, bf16[1024,512]{1,0:T(8,128)(2,1)}, u32[]{:S(2)}, u32[]{:S(2)}) %collective-permute-start.1) | collective-permute-done | bytes 1048608 | tf_op jit(solution)/shard_map/ppermute | solution.py:23
  50.9 2.7 %fusion.1 = f32[512,512]{0,1:T(8,128)} fusion(bf16[768,512]{1,0:T(8,128)(2,1)S(1)} %copy-done, bf16[1024,512]{1,0:T(8,128)(2,1)} %collective-permute-done.1), kind=kOutput, calls=%fused_computation.4 | convolution fusion | flops 402915328 | bytes 2621440 | tf_op jit(solution)/shard_map/dot_general | solution.py:48
  53.6 1.6 copy.19
  55.2 2.7 %fusion = f32[512,512]{0,1:T(8,128)} fusion(bf16[768,512]{1,0:T(8,128)(2,1)S(1)} %copy-done, bf16[1024,512]{1,0:T(8,128)(2,1)} %collective-permute-done.1), kind=kOutput, calls=%fused_computation.2 | convolution fusion | flops 402915328 | bytes 2621440 | tf_op jit(solution)/shard_map/dot_general | solution.py:48
  57.9 1.6 copy.21
  59.4 2.0 maximum_bitcast_fusion
  61.4 2.4 %copy.22 = f32[4,8,16,2,2,512]{5,2,4,3,1,0:T(8,128)} copy(f32[4,8,16,2,2,512]{5,2,0,1,4,3:T(8,128)S(1)} %maximum_bitcast_fusion) | data formatting | bytes 8388608 | tf_op jit(solution)/shard_map/transpose | solution.py:29
  63.8 0.0 reduce-scatter.3.cloned.1.call-update
  63.8 0.0 reduce-scatter.5.cloned.1.call-start
  63.9 87.8 %reduce-scatter.3.cloned.1.call-done = f32[8,16,2,2,512]{4,1,3,2,0:T(8,128)} async-done(((f32[32,16,2,2,512]{4,1,3,2,0:T(8,128)}), f32[8,16,2,2,512]{4,1,3,2,0:T(8,128)}) %reduce-scatter.3.cloned.1.call-update) | async-done | bytes 1048592 | tf_op jit(solution)/shard_map/reduce_scatter | solution.py:32
  151.6 0.0 reduce-scatter.5.cloned.1.call-update
  151.7 70.6 %reduce-scatter.5.cloned.1.call-done = f32[1,16,2,2,512]{4,1,3,2,0:T(8,128)} async-done(((f32[8,16,2,2,512]{4,1,3,2,0:T(8,128)}), f32[1,16,2,2,512]{4,1,3,2,0:T(8,128)}) %reduce-scatter.5.cloned.1.call-update) | async-done | bytes 131088 | tf_op jit(solution)/shard_map/reduce_scatter | solution.py:32
  222.3 0.9 slice_bitcast_fusion
  223.1 0.7 copy.24
  223.8 0.7 copy.23
Async XLA Ops:
  7.2 29.3 %copy-start = (bf16[768,512]{1,0:T(8,128)(2,1)S(1)}, bf16[768,512]{1,0:T(8,128)(2,1)}, u32[]{:S(2)}) copy-start(bf16[768,512]{1,0:T(8,128)(2,1)} %param.1) | copy-start | bytes 2359300
  7.2 144.5 %reduce-scatter.3.cloned.1.call-start = ((), (), s32[]{:S(2)}) async-start(), calls=%async_computation.2 | async-start | bytes 5242880 | tf_op jit(solution)/shard_map/reduce_scatter | solution.py:32
  8.3 9.9 %collective-permute-start = (bf16[256,512]{1,0:T(8,128)(2,1)S(1)}, bf16[256,512]{1,0:T(8,128)(2,1)S(1)}, u32[]{:S(2)}, u32[]{:S(2)}) collective-permute-start(bf16[256,512]{1,0:T(8,128)(2,1)S(1)} %slice.18), channel_id=1, source_target_pairs={{16,0},{32,16},{48,32},{64,48},{80,64},{96,80},{112,96},{128,112},... | collective-permute-start | bytes 786440 | tf_op jit(solution)/shard_map/ppermute | solution.py:18
  18.9 31.9 %collective-permute-start.1 = (bf16[1024,512]{1,0:T(8,128)(2,1)}, bf16[1024,512]{1,0:T(8,128)(2,1)}, u32[]{:S(2)}, u32[]{:S(2)}) collective-permute-start(bf16[1024,512]{1,0:T(8,128)(2,1)} %constant_dynamic-update-slice_fusion), channel_id=1, source_target_pairs={{0,15},{1,0},{2,1},{3,2},{4,3},{5,4},{6,5},{7,6},{8,7},{9,8},{10,9... | collective-permute-start | bytes 3145736 | tf_op jit(solution)/shard_map/ppermute | solution.py:23
  63.8 158.4 %reduce-scatter.5.cloned.1.call-start = ((), (), s32[]{:S(2)}) async-start(), calls=%async_computation.3 | async-start | bytes 1179648 | tf_op jit(solution)/shard_map/reduce_scatter | solution.py:32
Sparse Core Ops, SparseCore 0:
  64.0 87.6 reduce-scatter.2
  154.7 67.5 reduce-scatter.4
where the time goes:
time: 232 us; the launch traced here: 231 us
  waiting for transfers between devices  177 us (76%)
  starting transfers between devices  15.9 us (7%)
  between operations  14.1 us (6%)
  local copies, waits for them, and re-layouts  11.9 us (5%)
  matrix products  10.1 us (4%)
    reduce_scatter x2, waiting for transfers between devices, own_block(): parts = lax.psum_scatter(parts, axes[k], scatter_dimension=0, tiled=True)  158 us
    ppermute x1, starting transfers between devices, passed_along(): lax.ppermute(shard, axis, [(i, (i + by) % peers) for i in range(peers)])  14.5 us
    ppermute x1, waiting for transfers between devices, passed_along(): lax.ppermute(shard, axis, [(i, (i + by) % peers) for i in range(peers)])  12.3 us
    dot_general x4, matrix products, one_tile(): lax.dot_general(columns, other, dims, preferred_element_type=jnp.float32)  10.1 us
    ppermute x1, waiting for transfers between devices, shifted_2(): return lax.ppermute(shard, axis, pairs)  6.56 us
  transfers between devices with their start and end apart: 4, of which 4 were waited for; matrix products, arithmetic and copies ran while one was open for 3% of the time, Pallas kernels for 0%

commit v1 on v0

v1 whole, which is shorter than its diff:
```python
import functools
import math

import jax
import jax.numpy as jnp
from jax import lax
from jax.experimental import pallas as pl
from jax.experimental.pallas import tpu as pltpu
from jax.sharding import PartitionSpec as P

LAG = 256
ROWS = 768
WIDTH = 512
NC = 2
C = WIDTH // NC
UNITS = 2 * NC
NY = 4
PEAK = 2.0**8.4
MESH = pl.DeviceIdType.MESH


def encode(part, dst):
    n = part.shape[0]
    grouped = part.reshape(n // 32, 2, 16, part.shape[1])
    top = jnp.max(jnp.max(jnp.abs(grouped), axis=0), axis=1, keepdims=True)
    scale = jnp.maximum(top, 1e-36).astype(jnp.bfloat16)
    unit = grouped * (PEAK / scale.astype(jnp.float32))[None]
    third = unit * unit * unit
    sixth = third * third
    code = (sixth * sixth * third).reshape(n, part.shape[1])
    dst[pl.ds(0, n), :] = code.astype(jnp.bfloat16)
    wide = jnp.broadcast_to(scale.astype(jnp.float32), (2, 8, part.shape[1]))
    dst[pl.ds(n, 16), :] = wide.reshape(16, part.shape[1]).astype(jnp.bfloat16)


def decode(src):
    n, width = src.shape[0] - 16, src.shape[1]
    code = src[pl.ds(0, n), :].astype(jnp.float32)
    scale = src[pl.ds(n, 16), :].astype(jnp.float32).reshape(2, 8, width)[:, :1]
    size = jnp.exp2(jnp.log2(jnp.abs(code)) * (1.0 / 15.0))
    value = jnp.where(code > 0, size, jnp.where(code < 0, -size, 0.0))
    value = value.reshape(n // 32, 2, 16, width) * (scale * (1.0 / PEAK))[None]
    return value.reshape(n, width)


def kernel(
    norm_scale, count_tm, count_feat,
    a_hbm, inst_ref, lag_ref,
    panels, left, tail, acc, ysend, yrecv, z1send, z1recv, z2send, z2recv, z3send, z3recv, half1, half2, half3,
    load_sem, psend, precv, tsem, ysem_s, ysem_r, zsem_s, zsem_r,
):
    tm, feat = lax.axis_index("tm"), lax.axis_index("feat")
    zl, y = tm // NY, tm % NY
    b0, b1, b2 = zl % 2, (zl // 2) % 2, zl // 4
    before = (tm, (feat + count_feat - 1) % count_feat)
    after = (tm, (feat + 1) % count_feat)
    ypeer = [((zl * NY) + (y + j) % NY, feat) for j in range(NY)]
    zpeer = [
        ((zl + step * (1 - 2 * bit)) * NY + y, feat) for step, bit in ((1, b0), (2, b1), (4, b2))
    ]

    loads = [
        pltpu.make_async_copy(a_hbm.at[:, pl.ds(c * C, C)], panels.at[c], load_sem.at[c]) for c in range(NC)
    ]
    for load in loads:
        load.start()

    barrier = pltpu.get_barrier_semaphore()
    for peer in ypeer[1:] + zpeer + [after]:
        pl.semaphore_signal(barrier, inc=1, device_id=peer, device_id_type=MESH)

    @pl.when(tm > 0)
    def _():
        pl.semaphore_signal(barrier, inc=1, device_id=(tm - 1, feat), device_id_type=MESH)

    pl.semaphore_wait(barrier, 8 - (tm + 1) // count_tm)

    def pass_panel(c):
        return pltpu.make_async_remote_copy(
            src_ref=panels.at[c], dst_ref=panels.at[NC + c], send_sem=psend.at[c], recv_sem=precv.at[c],
            device_id=before, device_id_type=MESH,
        )

    def pass_tail(target):
        return pltpu.make_async_remote_copy(
            src_ref=a_hbm.at[pl.ds(ROWS - LAG, LAG)], dst_ref=tail, send_sem=tsem.at[0], recv_sem=tsem.at[1],
            device_id=target, device_id_type=MESH,
        )

    for c in range(NC):
        loads[c].wait()
        pass_panel(c).start()

    @pl.when(tm < count_tm - 1)
    def _():
        pass_tail((tm + 1, feat)).start()

    def row_of(block, owner_y):
        bits = (block % 2) * 4 + (block // 2 % 2) * 2 + block // 4
        return owner_y * 256 + bits * 32

    per = C // 128
    for j in range(WIDTH // 128):
        cols = panels[j // per, :, pl.ds((j % per) * 128, 128)].T
        for p in range(2):
            for owner in range(NY):
                at = row_of(2 * j + p, owner)
                piece = cols[p * 64 + owner * 16 : p * 64 + owner * 16 + 16]
                left[pl.ds(at, 16), :] = piece
                left[pl.ds(at + 16, 16), pl.ds(LAG, ROWS - LAG)] = piece[:, : ROWS - LAG]

    @pl.when(tm == 0)
    def _():
        tail[...] = jnp.zeros_like(tail)

    @pl.when(tm > 0)
    def _():
        pass_tail((tm, feat)).wait_recv()

    for j in range(WIDTH // 128):
        cols = tail[:, pl.ds(j * 128, 128)].T
        for p in range(2):
            for owner in range(NY):
                at = row_of(2 * j + p, owner)
                left[pl.ds(at + 16, 16), pl.ds(0, LAG)] = cols[p * 64 + owner * 16 : p * 64 + owner * 16 + 16]

    def pass_y(u, j):
        return pltpu.make_async_remote_copy(
            src_ref=ysend.at[u, j - 1], dst_ref=yrecv.at[u, j - 1], send_sem=ysem_s.at[u, j - 1],
            recv_sem=ysem_r.at[u, j - 1], device_id=ypeer[j], device_id_type=MESH,
        )

    def product(u, j):
        owner = (y + j) % NY
        rows = left[pl.ds(pl.multiple_of(owner * 256, 256), 256), :]
        return jnp.dot(rows, panels[u], preferred_element_type=jnp.float32)

    def multiply(u):
        if u >= NC:
            pass_panel(u - NC).wait_recv()
        for j in range(1, NY):
            encode(product(u, j), ysend.at[u, j - 1])
            pass_y(u, j).start()
        acc[u] = product(u, 0)

    def sum_y(u):
        for j in range(1, NY):
            pass_y(u, j).wait_recv()
            acc[u] += decode(yrecv.at[u, j - 1])

    def pass_z(u, k, src, dst):
        return pltpu.make_async_remote_copy(
            src_ref=src.at[u], dst_ref=dst.at[u], send_sem=zsem_s.at[u, k], recv_sem=zsem_r.at[u, k],
            device_id=zpeer[k], device_id_type=MESH,
        )

    def part(ref, u, bit, n):
        return ref[u, pl.ds(pl.multiple_of(bit * n, n), n), :]

    def z1(u):
        encode(part(acc, u, 1 - b0, 128), z1send.at[u])
        pass_z(u, 0, z1send, z1recv).start()

    def z2(u):
        pass_z(u, 0, z1send, z1recv).wait_recv()
        half1[u] = part(acc, u, b0, 128) + decode(z1recv.at[u])
        encode(part(half1, u, 1 - b1, 64), z2send.at[u])
        pass_z(u, 1, z2send, z2recv).start()

    def z3(u):
        pass_z(u, 1, z2send, z2recv).wait_recv()
        half2[u] = part(half1, u, b1, 64) + decode(z2recv.at[u])
        z3send[u] = part(half2, u, 1 - b2, 32)
        pass_z(u, 2, z3send, z3recv).start()

    def finish(u):
        pass_z(u, 2, z3send, z3recv).wait_recv()
        done = (part(half2, u, b2, 32) + z3recv[u]) * norm_scale
        s, at = u // NC, (u % NC) * C
        inst_ref[:, s, pl.ds(at, C)] = done[:16]
        lag_ref[:, s, pl.ds(at, C)] = done[16:]

    for u in range(UNITS):
        multiply(u)
        if u < UNITS - 1 and u > 0:
            sum_y(u - 1)
    for c in range(NC):
        pass_panel(c).wait_send()
    for u in range(UNITS):
        if u >= UNITS - 2:
            sum_y(u)
        z1(u)
    for step in (z2, z3, finish):
        for u in range(UNITS):
            step(u)

    for u in range(UNITS):
        for j in range(1, NY):
            pass_y(u, j).wait_send()
        pass_z(u, 0, z1send, z1recv).wait_send()
        pass_z(u, 1, z2send, z2recv).wait_send()
        pass_z(u, 2, z3send, z3recv).wait_send()

    @pl.when(tm < count_tm - 1)
    def _():
        pass_tail((tm + 1, feat)).wait_send()


def shards(count_tm, count_feat, frames):
    norm_scale = 1.0 / math.sqrt(ROWS * count_tm)
    f32, bf16, sem = jnp.float32, jnp.bfloat16, pltpu.SemaphoreType.DMA
    out = jax.ShapeDtypeStruct((16, 2, WIDTH), f32)
    return pl.pallas_call(
        functools.partial(kernel, norm_scale, count_tm, count_feat),
        out_shape=(out, out),
        in_specs=[pl.BlockSpec(memory_space=pl.ANY)],
        out_specs=(pl.BlockSpec(memory_space=pltpu.VMEM), pl.BlockSpec(memory_space=pltpu.VMEM)),
        scratch_shapes=[
            pltpu.VMEM((UNITS, ROWS, C), bf16),
            pltpu.VMEM((NY * 256, ROWS), bf16),
            pltpu.VMEM((LAG, WIDTH), bf16),
            pltpu.VMEM((UNITS, 256, C), f32),
            pltpu.VMEM((UNITS, NY - 1, 256 + 16, C), bf16),
            pltpu.VMEM((UNITS, NY - 1, 256 + 16, C), bf16),
            pltpu.VMEM((UNITS, 128 + 16, C), bf16),
            pltpu.VMEM((UNITS, 128 + 16, C), bf16),
            pltpu.VMEM((UNITS, 64 + 16, C), bf16),
            pltpu.VMEM((UNITS, 64 + 16, C), bf16),
            pltpu.VMEM((UNITS, 32, C), f32),
            pltpu.VMEM((UNITS, 32, C), f32),
            pltpu.VMEM((UNITS, 128, C), f32),
            pltpu.VMEM((UNITS, 64, C), f32),
            pltpu.VMEM((UNITS, 32, C), f32),
            sem((NC,)), sem((NC,)), sem((NC,)), sem((2,)),
            sem((UNITS, NY - 1)), sem((UNITS, NY - 1)), sem((UNITS, 3)), sem((UNITS, 3)),
        ],
        compiler_params=pltpu.CompilerParams(
            collective_id=0, has_side_effects=True, vmem_limit_bytes=40 * 1024 * 1024
        ),
        cost_estimate=pl.CostEstimate(
            flops=8 * WIDTH * WIDTH * ROWS, bytes_accessed=4 * ROWS * WIDTH, transcendentals=8 * WIDTH * WIDTH
        ),
    )(frames)


def solution(mesh):
    count_tm, count_feat = mesh.shape["tm"], mesh.shape["feat"]
    out = P(("feat", "tm"), None, None)
    return jax.shard_map(
        functools.partial(shards, count_tm, count_feat),
        mesh=mesh,
        in_specs=(P("tm", "feat"),),
        out_specs=(out, out),
        check_vma=False,
    )
```

time: 232 us -> 91.1 us (0.39)
  the two profiles are of different devices: /device:TPU:6 before, /device:TPU:8 now
where the time goes in v1:
time: 91.1 us; the launch traced here: 90.9 us
  Pallas kernels  87.9 us (96%)
  local copies, waits for them, and re-layouts  2.39 us (3%)
    pallas_call x1, Pallas kernels, shards(): pl.pallas_call(functools.partial(kernel, norm_scale, count_tm, count_feat...  87.9 us
    unnamed x4, local copies, waits for them, and re-layouts  2.39 us

profile of v1, /device:TPU:8, one launch (start us, length us, event | category | flops | bytes accessed | tf_op | source)
XLA Modules:
  0.0 90.9 jit_solution(6831649477747015069)
XLA Ops:
  0.6 0.0 copy-start
  0.6 1.1 %copy-done = bf16[768,512]{1,0:T(8,128)(2,1)S(1)} copy-done((bf16[768,512]{1,0:T(8,128)(2,1)S(1)}, bf16[768,512]{1,0:T(8,128)(2,1)}, u32[]{:S(2)}) %copy-start) | copy-done | bytes 786456
  1.8 87.9 %shard_map.30 = (f32[16,2,512]{2,1,0:T(2,128)S(1)}, f32[16,2,512]{2,1,0:T(2,128)S(1)}) custom-call(bf16[768,512]{1,0:T(8,128)(2,1)S(1)} %copy-done), custom_call_target="tpu_custom_call" | custom-call | flops 1610612736 | bytes 1572864 | tf_op jit(solution)/shard_map/pallas_call | solution.py:213
  89.7 0.6 copy.5
  90.3 0.6 copy.6
Async XLA Ops:
  0.6 1.1 %copy-start = (bf16[768,512]{1,0:T(8,128)(2,1)S(1)}, bf16[768,512]{1,0:T(8,128)(2,1)}, u32[]{:S(2)}) copy-start(bf16[768,512]{1,0:T(8,128)(2,1)} %a_hbm.1) | copy-start | bytes 2359300

commit v2 on v1

v2 whole, which is shorter than its diff:
```python
import functools
import math

import jax
import jax.numpy as jnp
from jax import lax
from jax.experimental import pallas as pl
from jax.experimental.pallas import tpu as pltpu
from jax.sharding import PartitionSpec as P

LAG = 256
ROWS = 768
WIDTH = 512
NC = 4
C = WIDTH // NC
UNITS = 2 * NC
NY = 4
HALF = ROWS // 2
PEAK = 2.0**8.4
GROUPS = ((0, 1, 2, 3), (4, 5, 6), (7,))
MESH = pl.DeviceIdType.MESH


def aligned(at, n):
    return at if isinstance(at, int) else pl.multiple_of(at, n)


def encode(piece, dst, at, g, scales):
    n = piece.shape[0]
    line = lax.broadcasted_iota(jnp.int32, (16, C), 0)
    piece = piece.reshape(n // 32, 2, 16, C)
    codes = []
    for kind in range(2):
        part = piece[:, kind]
        top = jnp.max(jnp.max(jnp.abs(part), axis=0), axis=0, keepdims=True)
        scale = jnp.maximum(top, 1e-36).astype(jnp.bfloat16).astype(jnp.float32)
        scales = jnp.where(line == 2 * g + kind, scale, scales)
        unit = part * (PEAK / scale)
        third = unit * unit * unit
        sixth = third * third
        codes.append(sixth * sixth * third)
    dst[pl.ds(aligned(at, 16), n), :] = jnp.stack(codes, axis=1).reshape(n, C).astype(jnp.bfloat16)
    return scales


def decode(code, scales, g):
    n = code.shape[0]
    code = code.astype(jnp.float32)
    line = lax.broadcasted_iota(jnp.int32, (16, C), 0)
    size = jnp.exp2(jnp.log2(jnp.abs(code)) * (1.0 / 15.0))
    value = jnp.where(code > 0, size, jnp.where(code < 0, -size, 0.0)).reshape(n // 32, 2, 16, C)
    kinds = []
    for kind in range(2):
        scale = jnp.sum(jnp.where(line == 2 * g + kind, scales, 0.0), axis=0, keepdims=True)
        kinds.append(value[:, kind] * (scale * (1.0 / PEAK)))
    return jnp.stack(kinds, axis=1).reshape(n, C)


def kernel(
    norm_scale, count_tm, count_feat,
    a_hbm, inst_ref, lag_ref,
    panels, transit, left, tail, acc, ysend, yrecv, zsend1, zsend2, zsend3, zrecv1, zrecv2, zrecv3, half1, half2,
    load_sem, psend, precv, rsend, rrecv, tsem, ysem_s, ysem_r, zsem_s, zsem_r,
):
    tm, feat = lax.axis_index("tm"), lax.axis_index("feat")
    zsend, zrecv = (zsend1, zsend2, zsend3), (zrecv1, zrecv2, zrecv3)
    zl, y = tm // NY, tm % NY
    b0, b1, b2 = zl % 2, (zl // 2) % 2, zl // 4
    core, zh, x4 = feat % 2, feat // 2 % 2, feat // 4 * 4
    z = zh * 8 + zl

    def at_z(far, first, unit):
        return ((far % 8) * NY + y, first + far // 8 * 2 + unit)

    up, down = (z + 4) % 16, (z + 12) % 16
    ends = (up, down)
    starts = (down, up)
    twin = (tm, feat + 1 - 2 * core)
    relays = [at_z(far, x4, 0) for far in ends]
    sources = [at_z(far, x4, 0) for far in starts]
    onward = [
        (far % 8 * NY + y, (x4 + near // 8 * 2 + count_feat - 1) % count_feat) for far, near in zip(ends, starts)
    ]
    next_x4 = (feat + 1) % count_feat // 4 * 4
    forwarders = [at_z(far, next_x4, 0) for far in starts]
    ypeer = [((zl * NY) + (y + j) % NY, feat) for j in range(NY)]
    zpeer = [
        ((zl + step * (1 - 2 * bit)) * NY + y, feat) for step, bit in ((1, b0), (2, b1), (4, b2))
    ]

    loads = [
        pltpu.make_async_copy(a_hbm.at[:, pl.ds(c * C, C)], panels.at[c], load_sem.at[c]) for c in range(NC)
    ]
    for load in loads:
        load.start()

    barrier = pltpu.get_barrier_semaphore()
    def greet(peers):
        for peer in peers:
            pl.semaphore_signal(barrier, inc=1, device_id=peer, device_id_type=MESH)

    greet(ypeer[1:] + zpeer)

    @pl.when(core == 0)
    def _():
        greet([twin] + sources)

    @pl.when(core == 1)
    def _():
        greet(forwarders)

    @pl.when(tm > 0)
    def _():
        greet([(tm - 1, feat)])

    pl.semaphore_wait(barrier, 11 - 3 * core - (tm + 1) // count_tm)

    def half(c, way):
        return panels.at[c, pl.ds(way * HALF, HALF)]

    def pass_near(c, way):
        return pltpu.make_async_remote_copy(
            src_ref=half(c, way), dst_ref=half(NC + c, way), send_sem=psend.at[c, way], recv_sem=precv.at[c, way],
            device_id=twin, device_id_type=MESH,
        )

    def pass_far(c, way):
        return pltpu.make_async_remote_copy(
            src_ref=half(c, way), dst_ref=transit.at[c, way], send_sem=psend.at[c, way], recv_sem=rrecv.at[c, way],
            device_id=relays[way], device_id_type=MESH,
        )

    def pass_on(c, way):
        return pltpu.make_async_remote_copy(
            src_ref=transit.at[c, way], dst_ref=half(NC + c, way), send_sem=rsend.at[c, way],
            recv_sem=precv.at[c, way], device_id=onward[way], device_id_type=MESH,
        )

    def relay(c):
        @pl.when(core == 0)
        def _():
            for way in range(2):
                pass_far(c, way).wait_recv()
                pass_on(c, way).start()

    def pass_tail(target):
        return pltpu.make_async_remote_copy(
            src_ref=a_hbm.at[pl.ds(ROWS - LAG, LAG)], dst_ref=tail, send_sem=tsem.at[0], recv_sem=tsem.at[1],
            device_id=target, device_id_type=MESH,
        )

    @pl.when(tm < count_tm - 1)
    def _():
        pass_tail((tm + 1, feat)).start()

    for c in range(NC):
        loads[c].wait()

        @pl.when(core == 0)
        def _():
            for way in range(2):
                pass_far(c, way).start()

        @pl.when(core == 1)
        def _():
            for way in range(2):
                pass_near(c, way).start()

    def row_of(block, owner_y):
        bits = (block % 2) * 4 + (block // 2 % 2) * 2 + block // 4
        return owner_y * 256 + bits * 32

    def spread(cols, j, store):
        for p in range(2):
            for owner in range(NY):
                at = pl.multiple_of(row_of(2 * j + p, owner), 32)
                store(at, cols[p * 64 + owner * 16 : p * 64 + owner * 16 + 16])

    def turn(j, _):
        def store(at, piece):
            left[pl.ds(at, 16), :] = piece
            left[pl.ds(at + 16, 16), pl.ds(LAG, ROWS - LAG)] = piece[:, : ROWS - LAG]

        spread(panels[j].T, j, store)
        return 0

    lax.fori_loop(0, NC, turn, 0)

    @pl.when(tm == 0)
    def _():
        tail[...] = jnp.zeros_like(tail)

    @pl.when(tm > 0)
    def _():
        pass_tail((tm, feat)).wait_recv()

    def turn_tail(j, _):
        def store(at, piece):
            left[pl.ds(at + 16, 16), pl.ds(0, LAG)] = piece

        spread(tail[:, pl.ds(pl.multiple_of(j * C, C), C)].T, j, store)
        return 0

    lax.fori_loop(0, NC, turn_tail, 0)

    def pass_y(u, j):
        return pltpu.make_async_remote_copy(
            src_ref=ysend.at[u, j - 1], dst_ref=yrecv.at[u, j - 1], send_sem=ysem_s.at[u, j - 1],
            recv_sem=ysem_r.at[u, j - 1], device_id=(zl * NY + (y + j) % NY, feat), device_id_type=MESH,
        )

    def product(u, j):
        owner = (y + j) % NY
        rows = left[pl.ds(pl.multiple_of(owner * 256, 256), 256), :]
        return jnp.dot(rows, panels[u], preferred_element_type=jnp.float32)

    none = jnp.zeros((16, C), jnp.float32)

    def multiply(u):
        def one(j, _):
            to = ysend.at[u, j - 1]
            to[pl.ds(256, 16), :] = encode(product(u, j), to, 0, 0, none).astype(jnp.bfloat16)
            pass_y(u, j).start()
            return 0

        lax.fori_loop(1, NY, one, 0)
        acc[u] = product(u, 0)

    def sum_y(u):
        def one(j, _):
            pass_y(u, j).wait_recv()
            came = yrecv.at[u, j - 1]
            acc[u] += decode(came[pl.ds(0, 256), :], came[pl.ds(256, 16), :].astype(jnp.float32), 0)
            return 0

        lax.fori_loop(1, NY, one, 0)

    def message(buffers, k, t):
        n, ahead = 128 >> k, sum(map(len, GROUPS[:t]))
        return buffers[k].at[pl.ds(ahead * n + 16 * t, len(GROUPS[t]) * n + 16)]

    def pass_z(k, t):
        return pltpu.make_async_remote_copy(
            src_ref=message(zsend, k, t), dst_ref=message(zrecv, k, t), send_sem=zsem_s.at[k, t],
            recv_sem=zsem_r.at[k, t], device_id=zpeer[k], device_id_type=MESH,
        )

    sums = (acc, half1, half2)
    bits = (b0, b1, b2)

    def part(k, u, bit):
        n = 128 >> k
        return sums[k][u, pl.ds(pl.multiple_of(bit * n, n), n), :]

    def give(k, t):
        n, count, to = 128 >> k, len(GROUPS[t]), message(zsend, k, t)

        def one(g, scales):
            return encode(part(k, GROUPS[t][0] + g, 1 - bits[k]), to, g * n, g, scales)

        to[pl.ds(count * n, 16), :] = lax.fori_loop(0, count, one, none).astype(jnp.bfloat16)
        pass_z(k, t).start()

    def take(k, t):
        n, count, came = 128 >> k, len(GROUPS[t]), message(zrecv, k, t)
        pass_z(k, t).wait_recv()
        scales = came[pl.ds(count * n, 16), :].astype(jnp.float32)

        def total(g):
            code = came[pl.ds(aligned(g * n, 16), n), :]
            return part(k, GROUPS[t][0] + g, bits[k]) + decode(code, scales, g)

        if k < 2:

            def one(g, _):
                sums[k + 1][GROUPS[t][0] + g] = total(g)
                return 0

            lax.fori_loop(0, count, one, 0)
        else:
            for g, u in enumerate(GROUPS[t]):
                s, at = u // NC, (u % NC) * C
                done = total(g) * norm_scale
                inst_ref[:, s, pl.ds(at, C)] = done[:16]
                lag_ref[:, s, pl.ds(at, C)] = done[16:]

    def z1(t):
        give(0, t)

    def z2(t):
        take(0, t)
        give(1, t)

    def z3(t):
        take(1, t)
        give(2, t)

    def finish(t):
        take(2, t)

    def gate(_):
        @pl.when(core == 0)
        def _():
            for c in range(NC):
                for way in range(2):
                    pass_on(c, way).wait_send()

    def own_tile(c, _):
        multiply(c)
        return 0

    def next_tile(c, _):
        for way in range(2):
            pass_near(c, way).wait_recv()
        multiply(NC + c)
        return 0

    def sum_before(c, _):
        def one(u, _):
            sum_y(u)
            return 0

        lax.fori_loop(jnp.minimum(2 * c, c + 2), jnp.minimum(2 * c + 2, c + 3), one, 0)
        return 0

    lax.fori_loop(0, NC, own_tile, 0)

    @pl.when(core == 0)
    def _():
        def pass_through(c, _):
            relay(c)
            return sum_before(c, 0)

        lax.fori_loop(0, NC, next_tile, 0)
        lax.fori_loop(0, NC, pass_through, 0)

    @pl.when(core == 1)
    def _():
        def wait_for_next(c, _):
            sum_before(c, 0)
            return next_tile(c, 0)

        lax.fori_loop(0, NC, wait_for_next, 0)

    z1(0)
    sum_y(6)
    z1(1)
    sum_y(7)
    z1(2)
    for step in (z2, z3, finish):
        for t in range(len(GROUPS)):
            step(t)

    gate(0)
    for c in range(NC):
        for way in range(2):
            pass_near(c, way).wait_send()

    for u in range(UNITS):
        for j in range(1, NY):
            pass_y(u, j).wait_send()
    for k in range(3):
        for t in range(len(GROUPS)):
            pass_z(k, t).wait_send()

    @pl.when(tm < count_tm - 1)
    def _():
        pass_tail((tm + 1, feat)).wait_send()


def shards(count_tm, count_feat, frames):
    norm_scale = 1.0 / math.sqrt(ROWS * count_tm)
    f32, bf16, sem = jnp.float32, jnp.bfloat16, pltpu.SemaphoreType.DMA
    out = jax.ShapeDtypeStruct((16, 2, WIDTH), f32)
    return pl.pallas_call(
        functools.partial(kernel, norm_scale, count_tm, count_feat),
        out_shape=(out, out),
        in_specs=[pl.BlockSpec(memory_space=pl.ANY)],
        out_specs=(pl.BlockSpec(memory_space=pltpu.VMEM), pl.BlockSpec(memory_space=pltpu.VMEM)),
        scratch_shapes=[
            pltpu.VMEM((UNITS, ROWS, C), bf16),
            pltpu.VMEM((NC, 2, HALF, C), bf16),
            pltpu.VMEM((NY * 256, ROWS), bf16),
            pltpu.VMEM((LAG, WIDTH), bf16),
            pltpu.VMEM((UNITS, 256, C), f32),
            pltpu.VMEM((UNITS, NY - 1, 256 + 16, C), bf16),
            pltpu.VMEM((UNITS, NY - 1, 256 + 16, C), bf16),
            *[pltpu.VMEM((UNITS * n + 16 * len(GROUPS), C), bf16) for n in (128, 64, 32)] * 2,
            pltpu.VMEM((UNITS, 128, C), f32),
            pltpu.VMEM((UNITS, 64, C), f32),
            sem((NC,)), sem((NC, 2)), sem((NC, 2)), sem((NC, 2)), sem((NC, 2)), sem((2,)),
            sem((UNITS, NY - 1)), sem((UNITS, NY - 1)), sem((3, len(GROUPS))), sem((3, len(GROUPS))),
        ],
        compiler_params=pltpu.CompilerParams(
            collective_id=0, has_side_effects=True, vmem_limit_bytes=40 * 1024 * 1024
        ),
        cost_estimate=pl.CostEstimate(
            flops=8 * WIDTH * WIDTH * ROWS, bytes_accessed=4 * ROWS * WIDTH, transcendentals=8 * WIDTH * WIDTH
        ),
    )(frames)


def solution(mesh):
    count_tm, count_feat = mesh.shape["tm"], mesh.shape["feat"]
    out = P(("feat", "tm"), None, None)
    return jax.shard_map(
        functools.partial(shards, count_tm, count_feat),
        mesh=mesh,
        in_specs=(P("tm", "feat"),),
        out_specs=(out, out),
        check_vma=False,
    )
```

time: 91.1 us -> 78 us (0.86)
  the two profiles are of different devices: /device:TPU:8 before, /device:TPU:1 now
where the time goes in v2:
time: 78 us; the launch traced here: 77.5 us
  Pallas kernels  74.4 us (95%)
  local copies, waits for them, and re-layouts  2.39 us (3%)
    pallas_call x1, Pallas kernels, shards(): pl.pallas_call(functools.partial(kernel, norm_scale, count_tm, count_feat...  74.4 us
    unnamed x4, local copies, waits for them, and re-layouts  2.39 us

profile of v2, /device:TPU:1, one launch (start us, length us, event | category | flops | bytes accessed | tf_op | source)
XLA Modules:
  0.0 77.5 jit_solution(11904161050676852622)
XLA Ops:
  0.6 0.0 copy-start
  0.6 1.1 %copy-done = bf16[768,512]{1,0:T(8,128)(2,1)S(1)} copy-done((bf16[768,512]{1,0:T(8,128)(2,1)S(1)}, bf16[768,512]{1,0:T(8,128)(2,1)}, u32[]{:S(2)}) %copy-start) | copy-done | bytes 786456
  1.8 74.4 %shard_map.30 = (f32[16,2,512]{2,1,0:T(2,128)S(1)}, f32[16,2,512]{2,1,0:T(2,128)S(1)}) custom-call(bf16[768,512]{1,0:T(8,128)(2,1)S(1)} %copy-done), custom_call_target="tpu_custom_call" | custom-call | flops 1610612736 | bytes 1572864 | tf_op jit(solution)/shard_map/pallas_call | solution.py:375
  76.2 0.6 copy.5
  76.8 0.6 copy.6
Async XLA Ops:
  0.6 1.1 %copy-start = (bf16[768,512]{1,0:T(8,128)(2,1)S(1)}, bf16[768,512]{1,0:T(8,128)(2,1)}, u32[]{:S(2)}) copy-start(bf16[768,512]{1,0:T(8,128)(2,1)} %a_hbm.1) | copy-start | bytes 2359300

commit v3 on v2

--- a/solution.py
+++ b/solution.py
@@ -305,6 +305,24 @@
                 for way in range(2):
                     pass_on(c, way).wait_send()
 
+    def early0(c):
+        @pl.when(c == 2)
+        def _():
+            z1(0)
+
+        @pl.when(c == 3)
+        def _():
+            z2(0)
+
+    def early1(c):
+        @pl.when(c == 1)
+        def _():
+            z1(0)
+
+        @pl.when(c == 2)
+        def _():
+            z2(0)
+
     def own_tile(c, _):
         multiply(c)
         return 0
@@ -329,7 +347,9 @@
     def _():
         def pass_through(c, _):
             relay(c)
-            return sum_before(c, 0)
+            sum_before(c, 0)
+            early0(c)
+            return 0
 
         lax.fori_loop(0, NC, next_tile, 0)
         lax.fori_loop(0, NC, pass_through, 0)
@@ -338,16 +358,19 @@
     def _():
         def wait_for_next(c, _):
             sum_before(c, 0)
-            return next_tile(c, 0)
+            next_tile(c, 0)
+            early1(c)
+            return 0
 
         lax.fori_loop(0, NC, wait_for_next, 0)
 
-    z1(0)
     sum_y(6)
     z1(1)
     sum_y(7)
     z1(2)
-    for step in (z2, z3, finish):
+    z2(1)
+    z2(2)
+    for step in (z3, finish):
         for t in range(len(GROUPS)):
             step(t)
 

time: 78 us -> 77 us (0.987)
  Pallas kernels: 74.4 us -> 73.6 us
    pallas_call x1, Pallas kernels: 74.4 us -> 73.6 us  [shards(): pl.pallas_call(functools.partial(kernel, norm_scale, count_tm, count_feat...]
where the time goes in v3:
time: 77 us; the launch traced here: 76.6 us
  Pallas kernels  73.6 us (96%)
  local copies, waits for them, and re-layouts  2.39 us (3%)
    pallas_call x1, Pallas kernels, shards(): pl.pallas_call(functools.partial(kernel, norm_scale, count_tm, count_feat...  73.6 us
    unnamed x4, local copies, waits for them, and re-layouts  2.39 us

profile of v3, /device:TPU:1, one launch (start us, length us, event | category | flops | bytes accessed | tf_op | source)
XLA Modules:
  0.0 76.6 jit_solution(16067073824782401886)
XLA Ops:
  0.6 0.0 copy-start
  0.6 1.1 %copy-done = bf16[768,512]{1,0:T(8,128)(2,1)S(1)} copy-done((bf16[768,512]{1,0:T(8,128)(2,1)S(1)}, bf16[768,512]{1,0:T(8,128)(2,1)}, u32[]{:S(2)}) %copy-start) | copy-done | bytes 786456
  1.8 73.6 %shard_map.30 = (f32[16,2,512]{2,1,0:T(2,128)S(1)}, f32[16,2,512]{2,1,0:T(2,128)S(1)}) custom-call(bf16[768,512]{1,0:T(8,128)(2,1)S(1)} %copy-done), custom_call_target="tpu_custom_call" | custom-call | flops 1610612736 | bytes 1572864 | tf_op jit(solution)/shard_map/pallas_call | solution.py:398
  75.4 0.6 copy.5
  76.0 0.6 copy.6
Async XLA Ops:
  0.6 1.1 %copy-start = (bf16[768,512]{1,0:T(8,128)(2,1)S(1)}, bf16[768,512]{1,0:T(8,128)(2,1)}, u32[]{:S(2)}) copy-start(bf16[768,512]{1,0:T(8,128)(2,1)} %a_hbm.1) | copy-start | bytes 2359300

commit v4 on v3

--- a/solution.py
+++ b/solution.py
@@ -118,15 +118,18 @@
     def half(c, way):
         return panels.at[c, pl.ds(way * HALF, HALF)]
 
+    def origin(c, way):
+        return a_hbm.at[pl.ds(way * HALF, HALF), pl.ds(c * C, C)]
+
     def pass_near(c, way):
         return pltpu.make_async_remote_copy(
-            src_ref=half(c, way), dst_ref=half(NC + c, way), send_sem=psend.at[c, way], recv_sem=precv.at[c, way],
+            src_ref=origin(c, way), dst_ref=half(NC + c, way), send_sem=psend.at[c, way], recv_sem=precv.at[c, way],
             device_id=twin, device_id_type=MESH,
         )
 
     def pass_far(c, way):
         return pltpu.make_async_remote_copy(
-            src_ref=half(c, way), dst_ref=transit.at[c, way], send_sem=psend.at[c, way], recv_sem=rrecv.at[c, way],
+            src_ref=origin(c, way), dst_ref=transit.at[c, way], send_sem=psend.at[c, way], recv_sem=rrecv.at[c, way],
             device_id=relays[way], device_id_type=MESH,
         )
 
@@ -154,7 +157,6 @@
         pass_tail((tm + 1, feat)).start()
 
     for c in range(NC):
-        loads[c].wait()
 
         @pl.when(core == 0)
         def _():
@@ -165,6 +167,9 @@
         def _():
             for way in range(2):
                 pass_near(c, way).start()
+
+    for load in loads:
+        load.wait()
 
     def row_of(block, owner_y):
         bits = (block % 2) * 4 + (block // 2 % 2) * 2 + block // 4

time: 77 us -> 76.8 us (level)
  no operation moved by 1% of the time
where the time goes in v4:
time: 76.8 us; the launch traced here: 76.6 us
  Pallas kernels  73.6 us (96%)
  local copies, waits for them, and re-layouts  2.39 us (3%)
    pallas_call x1, Pallas kernels, shards(): pl.pallas_call(functools.partial(kernel, norm_scale, count_tm, count_feat...  73.6 us
    unnamed x4, local copies, waits for them, and re-layouts  2.39 us

profile of v4, /device:TPU:1, one launch (start us, length us, event | category | flops | bytes accessed | tf_op | source)
XLA Modules:
  0.0 76.6 jit_solution(14621955404134932192)
XLA Ops:
  0.6 0.0 copy-start
  0.6 1.1 %copy-done = bf16[768,512]{1,0:T(8,128)(2,1)S(1)} copy-done((bf16[768,512]{1,0:T(8,128)(2,1)S(1)}, bf16[768,512]{1,0:T(8,128)(2,1)}, u32[]{:S(2)}) %copy-start) | copy-done | bytes 786456
  1.8 73.6 %shard_map.30 = (f32[16,2,512]{2,1,0:T(2,128)S(1)}, f32[16,2,512]{2,1,0:T(2,128)S(1)}) custom-call(bf16[768,512]{1,0:T(8,128)(2,1)S(1)} %copy-done), custom_call_target="tpu_custom_call" | custom-call | flops 1610612736 | bytes 1572864 | tf_op jit(solution)/shard_map/pallas_call | solution.py:403
  75.4 0.6 copy.5
  76.0 0.6 copy.6
Async XLA Ops:
  0.6 1.1 %copy-start = (bf16[768,512]{1,0:T(8,128)(2,1)S(1)}, bf16[768,512]{1,0:T(8,128)(2,1)}, u32[]{:S(2)}) copy-start(bf16[768,512]{1,0:T(8,128)(2,1)} %a_hbm.1) | copy-start | bytes 2359300
